TPU v7x, 32 devices: a whole 2x2x4 slice. The times are simulated.
32 devices in a mesh: tower: 4 (over y, x), intra: 8 (over z, core).
Axes of the slice: x: 2, y: 2, z: 4, core: 2. Of those that a mesh axis runs over, the one named last changes fastest.
Arguments:
- embeddings: bfloat16 [256, 16384], P(None, ('tower', 'intra')), may hold values from -6 to 6
- feature_assign: int32 [4, 32], P('tower'), may hold values from 0 to 31, each once within a row
- sample_owner: int32 [256], replicated, may hold values from 0 to 255, each once
- first_weight: bfloat16 [8, 2048, 1024], P('tower'), may hold values from -0.125 to 0.125
- first_bias: float32 [8, 1024], P('tower'), may hold values from -3 to 3
- tower_weight: bfloat16 [8, 1024, 256], P('tower'), may hold values from -0.1875 to 0.1875
- tower_bias: float32 [8, 256], P('tower'), may hold values from -3 to 3
- proj_weight: bfloat16 [16, 128], replicated, may hold values from -1.5 to 1.5
Outputs:
- interaction: bfloat16 [256, 16, 128], P(('tower', 'intra'))
Inputs may be any that keep to these rules, and one draw needn't show every extreme that they name: `feature_assign`: each row is a permutation of 0 to 31. `sample_owner`: a permutation of 0 to 255.
All inputs are finite; a program needn't handle non-finite values.
Results may differ from a plain program's by a relative error of at most 0.0034.
Values may be sent and summed in bfloat16 or wider, within the bound.
No kernel may reach another device: no remote copies, remote signals or barrier semaphores. Data moves between devices by JAX's collectives and lax.ppermute only.
A program may use at most 64 MiB of HBM per device.

v0:
```python
import jax
import jax.numpy as jnp
from jax import lax
from jax.sharding import PartitionSpec as P

EDIM = 128
TOW_DEV = 2
TIN = 2048
TVEC = 2
FPT = 32


def shards(
    embeddings,
    feature_assign,
    sample_owner,
    first_weight,
    first_bias,
    tower_weight,
    tower_bias,
    proj_weight,
):
    tower_count = lax.axis_size("tower")
    intra_count = lax.axis_size("intra")
    samples = embeddings.shape[0]
    per_device = samples // (tower_count * intra_count)
    block_rows = per_device * tower_count
    sample_order = (
        sample_owner.reshape(tower_count, intra_count, per_device).transpose(1, 0, 2).reshape(-1)
    )
    ordered = jnp.take(embeddings, sample_order, axis=0)
    outgoing = ordered.reshape(intra_count, block_rows, embeddings.shape[1])
    assign_row = feature_assign[0]
    received = lax.all_to_all(outgoing, "intra", split_axis=0, concat_axis=2, tiled=True)
    count = received.shape[1]
    features = received.reshape(count, FPT, EDIM)
    features = jnp.take(features, assign_row, axis=1)
    inputs = features.reshape(count, TOW_DEV, TIN)
    hidden = jnp.einsum("nkc,kch->nkh", inputs, first_weight, preferred_element_type=jnp.float32)
    hidden = jnp.maximum(hidden + first_bias[None, :, :], 0.0).astype(jnp.bfloat16)
    result = jnp.einsum("nkh,kho->nko", hidden, tower_weight, preferred_element_type=jnp.float32)
    result = result + tower_bias[None, :, :]
    vectors = jnp.maximum(result, 0.0).astype(jnp.bfloat16).reshape(count, TOW_DEV * TVEC, EDIM)
    owned = lax.all_to_all(vectors, "tower", split_axis=0, concat_axis=1, tiled=True)
    gram_matrix = (
        jnp.einsum("pie,pje->pij", owned, owned, preferred_element_type=jnp.float32) / EDIM
    )
    result = jnp.einsum(
        "pij,je->pie", gram_matrix, proj_weight.astype(jnp.float32), precision=lax.Precision.HIGHEST
    )
    return result.astype(jnp.bfloat16)


def solution(mesh):
    return jax.shard_map(
        shards,
        mesh=mesh,
        in_specs=(
            P(None, ("tower", "intra")),
            P("tower", None),
            P(),
            P("tower", None, None),
            P("tower", None),
            P("tower", None, None),
            P("tower", None),
            P(),
        ),
        out_specs=P(("tower", "intra"), None, None),
        check_vma=False,
    )
```

profile of v0, /device:TPU:0, one launch (start us, length us, event | category | flops | bytes accessed | tf_op | source)
XLA Modules:
  0.0 36.0 jit_solution(16524927216677164785)
XLA Ops:
  0.0 0.8 %reshape.98 = s32[4,8,8]{2,1,0:T(8,128)S(1)} reshape(s32[256]{0:T(256)} %param.10) | data formatting | bytes 2048 | tf_op jit(solution)/shard_map/reshape | solution.py:29
  0.9 0.1 reshape.100
  1.0 0.1 reshape.99
  1.1 0.0 copy-start.1
  1.1 2.2 %gather_fusion = bf16[256,512]{1,0:T(8,128)(2,1)S(1)} fusion(bf16[256,512]{1,0:T(8,128)(2,1)} %param.8, s32[1024]{0:T(1024)S(1)} %pad_clamp_fusion.1), kind=kCustom, calls=%fused_computation | custom fusion | bytes 525312 | tf_op jit(solution)/shard_map/jit(_take)/gather | solution.py:31
  3.3 0.8 %broadcast_select_fusion.1 = bf16[8,32,512]{2,1,0:T(8,128)(2,1)} fusion(bf16[8,32,512]{2,1,0:T(8,128)(2,1)S(1)} %bitcast.42, pred[8,32]{1,0:T(8,128)(4,1)S(1)} %compare_and_fusion), kind=kLoop, calls=%fused_computation.15 | loop fusion | flops 131072 | bytes 524544 | tf_op jit(solution)/shard_map/jit(_take)/select_n | solution.py:31
  4.1 6.3 %all-to-all-start = ((bf16[8,32,512]{2,1,0:T(8,128)(2,1)}), bf16[8,32,512]{2,1,0:T(8,128)(2,1)S(1)}, u32[]{:S(2)}, u32[]{:S(2)}) async-start(bf16[8,32,512]{2,1,0:T(8,128)(2,1)} %broadcast_select_fusion.1), calls=%async_computation | async-start | bytes 524288 | tf_op jit(solution)/shard_map/all_to_all | solution.py:34
  10.4 0.5 %broadcast.83 = s32[]{:T(128)} broadcast(s32[]{:T(128)} %constant.69), dimensions={} | broadcast | bytes 8 | tf_op args[1]
  10.9 1.3 %reduce.3 = s32[32]{0:T(128)S(1)} reduce(s32[1,32]{1,0:T(1,128)} %param.9, s32[]{:T(128)} %broadcast.83), dimensions={0}, to_apply=%param.9.reduce_sub_computation.3 | reduce | bytes 260 | tf_op args[1]
  12.2 0.1 squeeze.5
  12.3 0.1 broadcast_bitcast_fusion
  12.4 0.7 %fusion.14 = s32[32]{0:T(128)S(1)} fusion(s32[1,32]{1,0:T(1,128)} %param.9), kind=kLoop, calls=%fused_computation.30 | loop fusion | flops 96 | bytes 256 | tf_op jit(solution)/shard_map/jit(_take)/jit(_where)/select_n | solution.py:37
  13.1 7.1 %all-to-all-done = bf16[8,32,512]{2,1,0:T(8,128)(2,1)S(1)} async-done(((bf16[8,32,512]{2,1,0:T(8,128)(2,1)}), bf16[8,32,512]{2,1,0:T(8,128)(2,1)S(1)}, u32[]{:S(2)}, u32[]{:S(2)}) %all-to-all-start) | async-done | bytes 262176 | tf_op jit(solution)/shard_map/all_to_all | solution.py:34
  20.2 0.1 copy.26
  20.3 0.2 reshape.101
  20.5 0.1 copy.27
  20.6 0.6 %gather_fusion.1 = bf16[32,32,128]{2,1,0:T(8,128)(2,1)S(1)} fusion(bf16[32,32,128]{2,0,1:T(8,128)(2,1)S(1)} %copy.27, s32[1024]{0:T(1024)S(1)} %pad_clamp_fusion), kind=kCustom, calls=%fused_computation.1 | custom fusion | bytes 524416 | tf_op jit(solution)/shard_map/jit(_take)/gather | solution.py:37
  21.2 0.1 copy.28
  21.3 0.1 gather.15
  21.4 0.2 broadcast_select_fusion
  21.6 5.1 %fusion.7 = bf16[32,2,256]{2,0,1:T(8,128)(2,1)S(1)} fusion(bf16[2,1024,256]{2,1,0:T(8,128)(2,1)S(1)} %copy-done, bf16[2,2048,1024]{2,1,0:T(8,128)(2,1)} %param.11, bf16[32,2,2048]{2,1,0:T(2,128)(2,1)S(1)} %broadcast_select_fusion, f32[2,1024]{1,0:T(2,128)} %param.12, f32[2,256]{1,0:T(2,128)} %param.14), kind=kOutput, calls=%fused_computation.12 | convolution fusion | flops 302235648 | bytes 9742336 | tf_op jit(solution)/shard_map/nkh,kho->nko/dot_general | solution.py:41
  26.8 8.3 %all_to_all.33 = bf16[32,4,128]{2,1,0:T(4,128)(2,1)S(1)} all-to-all(bf16[32,4,128]{2,1,0:T(4,128)(2,1)S(1)} %reshape.102), channel_id=1, replica_groups=mesh['tower'=4,'intra'=8] {'tower'}, dimensions={0} | all-to-all | bytes 65536 | tf_op jit(solution)/shard_map/all_to_all | solution.py:44
  35.1 0.1 convolution_multiply_fusion
  35.2 0.8 %convolution_convert_fusion = bf16[8,16,128]{2,1,0:T(8,128)(2,1)} fusion(f32[8,16,16]{2,1,0:T(8,128)S(1)} %convolution_multiply_fusion, bf16[16,128]{1,0:T(8,128)(2,1)S(1)} %copy-done.1), kind=kOutput, calls=%fused_computation.11 | convolution fusion | flops 3162112 | bytes 45056 | tf_op jit(solution)/shard_map/pij,je->pie/dot_general | solution.py:48
  (13 shorter events, 0.1 us)
Async XLA Ops:
  0.0 21.6 %copy-start = (bf16[2,1024,256]{2,1,0:T(8,128)(2,1)S(1)}, bf16[2,1024,256]{2,1,0:T(8,128)(2,1)}, u32[]{:S(2)}) copy-start(bf16[2,1024,256]{2,1,0:T(8,128)(2,1)} %param.13) | copy-start | bytes 3145732
  1.1 34.1 %copy-start.1 = (bf16[16,128]{1,0:T(8,128)(2,1)S(1)}, bf16[16,128]{1,0:T(8,128)(2,1)}, u32[]{:S(2)}) copy-start(bf16[16,128]{1,0:T(8,128)(2,1)} %param.15) | copy-start | bytes 12292
  4.1 16.1 %all-to-all-start = ((bf16[8,32,512]{2,1,0:T(8,128)(2,1)}), bf16[8,32,512]{2,1,0:T(8,128)(2,1)S(1)}, u32[]{:S(2)}, u32[]{:S(2)}) async-start(bf16[8,32,512]{2,1,0:T(8,128)(2,1)} %broadcast_select_fusion.1), calls=%async_computation | async-start | bytes 524288 | tf_op jit(solution)/shard_map/all_to_all | solution.py:34
where the time goes:
time: 36.3 us; the launch traced here: 36 us
  blocking collectives  8.27 us (23%)
  waiting for transfers between devices  7.05 us (19%)
  starting transfers between devices  6.33 us (17%)
  matrix products  5.98 us (16%)
  local copies, waits for them, and re-layouts  5.19 us (14%)
  other arithmetic  3.05 us (8%)
    all_to_all x1, blocking collectives, shards(): lax.all_to_all(vectors, 'tower', split_axis=0, concat_axis=1, tiled=True)  8.27 us
    all_to_all x1, waiting for transfers between devices, shards(): lax.all_to_all(outgoing, 'intra', split_axis=0, concat_axis=2, tiled=True)  7.05 us
    all_to_all x1, starting transfers between devices, shards(): lax.all_to_all(outgoing, 'intra', split_axis=0, concat_axis=2, tiled=True)  6.33 us
    dot_general x1, matrix products, shards(): jnp.einsum('nkh,kho->nko', hidden, tower_weight, preferred_element_type=j...  5.08 us
    gather x1, local copies, waits for them, and re-layouts, shards(): ordered = jnp.take(embeddings, sample_order, axis=0)  2.2 us
    unnamed x1, other arithmetic  1.32 us
    reshape x3, local copies, waits for them, and re-layouts, shards(): sample_owner.reshape(tower_count, intra_count, per_device)  1.02 us
    select_n x2, other arithmetic, shards(): features = jnp.take(features, assign_row, axis=1)  0.9 us
  transfers between devices with their start and end apart: 1, of which 1 were waited for; matrix products, arithmetic and copies ran while one was open for 7% of the time, Pallas kernels for 0%

commit v1 on v0

v1 whole, which is shorter than its diff:
```python
import functools

import jax
import jax.numpy as jnp
from jax import lax
from jax.experimental import pallas as pl
from jax.experimental.pallas import tpu as pltpu
from jax.sharding import PartitionSpec as P

EDIM = 128
FEW_SAMPLES = 1024


def swap(block, axis, size, offset):
    if offset == 0:
        return block
    return lax.ppermute(block, axis, [(i, i ^ offset) for i in range(size)])


def gather_kernel(towers, intra, owner_ref, emb_ref, *rest):
    outs, acc_ref = rest[:intra], rest[intra]
    samples, width = emb_ref.shape
    per = samples // (towers * intra)
    me = lax.axis_index("intra")
    owner = jnp.broadcast_to(owner_ref[...].reshape(1, samples), (samples, samples))
    picks = lax.broadcasted_iota(jnp.int32, (samples, samples), 0) == owner
    picks = jnp.where(picks, 1.0, 0.0).astype(jnp.bfloat16)
    acc_ref[...] = lax.dot_general(
        picks, emb_ref[...], (((0,), (0,)), ((), ())), preferred_element_type=jnp.float32
    )
    for o, out in enumerate(outs):
        block = me ^ o
        starts = [pl.multiple_of((t * intra + block) * per, per) for t in range(towers)]
        for f in range(width // EDIM):
            columns = slice(f * EDIM, (f + 1) * EDIM)
            rows = [acc_ref[pl.ds(start, per), columns] for start in starts]
            out[f] = jnp.concatenate(rows, axis=0).astype(out.dtype)


def gather_blocks(owner, embeddings, towers, intra):
    samples, width = embeddings.shape
    rows, held = samples // intra, width // EDIM
    shape = jax.ShapeDtypeStruct((held, rows, EDIM), embeddings.dtype)
    if samples <= FEW_SAMPLES:
        return pl.pallas_call(
            functools.partial(gather_kernel, towers, intra),
            out_shape=[shape] * intra,
            in_specs=[pl.BlockSpec(memory_space=pltpu.VMEM)] * 2,
            out_specs=[pl.BlockSpec(memory_space=pltpu.VMEM)] * intra,
            scratch_shapes=[pltpu.VMEM((samples, width), jnp.float32)],
            compiler_params=pltpu.CompilerParams(vmem_limit_bytes=8 << 20),
            name="gather_rows",
        )(owner, embeddings)
    order = owner.reshape(towers, intra, -1).transpose(1, 0, 2).reshape(-1)
    blocks = jnp.take(embeddings, order, axis=0).reshape(intra, rows, held, EDIM).transpose(0, 2, 1, 3)
    me = lax.axis_index("intra")
    return [lax.dynamic_index_in_dim(blocks, me ^ o, keepdims=False) for o in range(intra)]


def tower_kernel(towers, intra, assign_ref, w1_ref, b1_ref, w2_ref, b2_ref, *rest):
    blocks, outs = rest[:intra], rest[intra : intra + towers]
    pool_ref, x_ref, y_ref = rest[intra + towers :]
    held, rows, _ = blocks[0].shape
    count, depth, _ = w1_ref.shape
    vectors = w2_ref.shape[2] // EDIM
    per = rows // towers
    slots = depth // EDIM
    me = lax.axis_index("intra")
    for o, block in enumerate(blocks):
        pool_ref[pl.ds((me ^ o) * held, held)] = block[...]
    for k in range(count):
        for j in range(slots):
            x_ref[k, :, j * EDIM : (j + 1) * EDIM] = pool_ref[assign_ref[0, k * slots + j]]
    for k in range(count):
        hidden = jnp.dot(x_ref[k], w1_ref[k], preferred_element_type=jnp.float32)
        hidden = jnp.maximum(hidden + b1_ref[k : k + 1, :], 0.0).astype(jnp.bfloat16)
        result = jnp.dot(hidden, w2_ref[k], preferred_element_type=jnp.float32)
        y_ref[k] = jnp.maximum(result + b2_ref[k : k + 1, :], 0.0)
    place = lax.axis_index("tower")
    for o, out in enumerate(outs):
        start = pl.multiple_of((place ^ o) * per, per)
        pieces = [
            y_ref[k, pl.ds(start, per), v * EDIM : (v + 1) * EDIM]
            for k in range(count)
            for v in range(vectors)
        ]
        out[...] = jnp.concatenate(pieces, axis=0).astype(out.dtype)


def run_towers(assign, w1, b1, w2, b2, blocks, towers):
    intra = len(blocks)
    held, rows, _ = blocks[0].shape
    count, depth, _ = w1.shape
    width = w2.shape[2]
    local = count * (width // EDIM) * (rows // towers)
    w1 = pltpu.with_memory_space_constraint(w1, pltpu.VMEM)
    w2 = pltpu.with_memory_space_constraint(w2, pltpu.VMEM)
    return pl.pallas_call(
        functools.partial(tower_kernel, towers, intra),
        out_shape=[jax.ShapeDtypeStruct((local, EDIM), jnp.bfloat16)] * towers,
        in_specs=[pl.BlockSpec(memory_space=pltpu.SMEM)]
        + [pl.BlockSpec(memory_space=pltpu.VMEM)] * (4 + intra),
        out_specs=[pl.BlockSpec(memory_space=pltpu.VMEM)] * towers,
        scratch_shapes=[
            pltpu.VMEM((intra * held, rows, EDIM), jnp.bfloat16),
            pltpu.VMEM((count, rows, depth), jnp.bfloat16),
            pltpu.VMEM((count, rows, width), jnp.float32),
        ],
        compiler_params=pltpu.CompilerParams(vmem_limit_bytes=16 << 20),
        name="towers",
    )(assign, w1, b1, w2, b2, *blocks)


def interact_kernel(towers, proj_ref, *rest):
    blocks, out, all_ref = rest[:towers], rest[towers], rest[towers + 1]
    per, count, _ = out.shape
    local = blocks[0].shape[0]
    place = lax.axis_index("tower")
    for o, block in enumerate(blocks):
        start = pl.multiple_of((place ^ o) * local, local)
        all_ref[pl.ds(start, local), :] = block[...].astype(jnp.float32)
    group = max(1, min(per, 128 // count))
    proj = jnp.concatenate([proj_ref[...]] * (2 * group), axis=0)
    for first in range(0, per, group):
        samples = range(first, first + group)
        vectors = [all_ref[pl.ds(d, count, stride=per), :] for d in samples]
        vectors = jnp.concatenate(vectors, axis=0).astype(jnp.bfloat16)
        gram = lax.dot_general(
            vectors, vectors, (((1,), (1,)), ((), ())), preferred_element_type=jnp.float32
        )
        gram = gram * (1.0 / EDIM)
        column = lax.broadcasted_iota(jnp.int32, (count, gram.shape[1]), 1)
        own = [
            jnp.where(
                (column >= g * count) & (column < (g + 1) * count),
                gram[g * count : (g + 1) * count, :],
                0.0,
            )
            for g in range(group)
        ]
        gram = jnp.concatenate(own, axis=0)
        high = gram.astype(jnp.bfloat16)
        low = (gram - high.astype(jnp.float32)).astype(jnp.bfloat16)
        result = jnp.dot(
            jnp.concatenate([high, low], axis=1), proj, preferred_element_type=jnp.float32
        )
        for g, d in enumerate(samples):
            out[d] = result[g * count : (g + 1) * count, :].astype(out.dtype)


def interact(proj, blocks):
    towers = len(blocks)
    local = blocks[0].shape[0]
    count = proj.shape[0]
    per = towers * local // count
    return pl.pallas_call(
        functools.partial(interact_kernel, towers),
        out_shape=jax.ShapeDtypeStruct((per, count, EDIM), jnp.bfloat16),
        in_specs=[pl.BlockSpec(memory_space=pltpu.VMEM)] * (1 + towers),
        out_specs=pl.BlockSpec(memory_space=pltpu.VMEM),
        scratch_shapes=[pltpu.VMEM((towers * local, EDIM), jnp.float32)],
        compiler_params=pltpu.CompilerParams(vmem_limit_bytes=8 << 20),
        name="interact",
    )(proj, *blocks)


def shards(
    embeddings,
    feature_assign,
    sample_owner,
    first_weight,
    first_bias,
    tower_weight,
    tower_bias,
    proj_weight,
):
    towers, intra = lax.axis_size("tower"), lax.axis_size("intra")
    blocks = gather_blocks(sample_owner, embeddings, towers, intra)
    blocks = [swap(block, "intra", intra, o) for o, block in enumerate(blocks)]
    vectors = run_towers(
        feature_assign, first_weight, first_bias, tower_weight, tower_bias, blocks, towers
    )
    vectors = [swap(block, "tower", towers, o) for o, block in enumerate(vectors)]
    return interact(proj_weight, vectors)


def solution(mesh):
    return jax.shard_map(
        shards,
        mesh=mesh,
        in_specs=(
            P(None, ("tower", "intra")),
            P("tower", None),
            P(),
            P("tower", None, None),
            P("tower", None),
            P("tower", None, None),
            P("tower", None),
            P(),
        ),
        out_specs=P(("tower", "intra"), None, None),
        check_vma=False,
    )
```

time: 36.3 us -> 34.5 us (0.950)
  blocking collectives: 8.27 us -> 0 us
  starting transfers between devices: 6.33 us -> 13.3 us
  matrix products: 5.98 us -> 0 us
  Pallas kernels: 0 us -> 3.51 us
  local copies, waits for them, and re-layouts: 5.19 us -> 8.27 us
  other arithmetic: 3.05 us -> 0 us
  waiting for transfers between devices: 7.05 us -> 9.09 us
    ppermute x0 -> x10, starting transfers between devices: none -> 13.3 us  [swap(): return lax.ppermute(block, axis, [(i, i ^ offset) for i in range(size)])]
    ppermute x0 -> x10, waiting for transfers between devices: none -> 9.09 us  [swap(): return lax.ppermute(block, axis, [(i, i ^ offset) for i in range(size)])]
    all_to_all x1 -> x0, blocking collectives: 8.27 us -> none  [shards(): lax.all_to_all(vectors, 'tower', split_axis=0, concat_axis=1, tiled=True)]
    unnamed x7 -> x16, local copies, waits for them, and re-layouts: 0.61 us -> 8.27 us
    all_to_all x1 -> x0, waiting for transfers between devices: 7.05 us -> none  [shards(): lax.all_to_all(outgoing, 'intra', split_axis=0, concat_axis=2, tiled=True)]
    all_to_all x1 -> x0, starting transfers between devices: 6.33 us -> none  [shards(): lax.all_to_all(outgoing, 'intra', split_axis=0, concat_axis=2, tiled=True)]
    dot_general x3 -> x0, matrix products: 5.98 us -> none  [the longest x1 5.08 us: shards(): jnp.einsum('nkh,kho->nko', hidden, tower_weight, preferred_element_type=j...]
    pallas_call x0 -> x3, Pallas kernels: none -> 3.51 us  [the longest x1 2.29 us: run_towers(): pl.pallas_call(functools.partial(tower_kernel, towers, intra), out_shape=...]
  transfers between devices with their start and end apart: 1 -> 10, of which waited for: 1 -> 6; matrix products, arithmetic and copies ran while one was open for 7% -> 0% of each run, Pallas kernels for 0% -> 0%
where the time goes in v1:
time: 34.5 us; the launch traced here: 34.2 us
  starting transfers between devices  13.3 us (39%)
  waiting for transfers between devices  9.09 us (26%)
  local copies, waits for them, and re-layouts  8.27 us (24%)
  Pallas kernels  3.51 us (10%)
    ppermute x10, starting transfers between devices, swap(): return lax.ppermute(block, axis, [(i, i ^ offset) for i in range(size)])  13.3 us
    ppermute x10, waiting for transfers between devices, swap(): return lax.ppermute(block, axis, [(i, i ^ offset) for i in range(size)])  9.09 us
    unnamed x16, local copies, waits for them, and re-layouts  8.27 us
    pallas_call x1, Pallas kernels, run_towers(): pl.pallas_call(functools.partial(tower_kernel, towers, intra), out_shape=...  2.29 us
    pallas_call x1, Pallas kernels, interact(): pl.pallas_call(functools.partial(interact_kernel, towers), out_shape=jax....  0.94 us
  transfers between devices with their start and end apart: 10, of which 6 were waited for; matrix products, arithmetic and copies ran while one was open for 0% of the time, Pallas kernels for 0%

profile of v1, /device:TPU:0, one launch (start us, length us, event | category | flops | bytes accessed | tf_op | source)
XLA Modules:
  0.0 34.2 jit_solution(1492253747651681783)
XLA Ops:
  0.0 0.9 %copy-done.2 = bf16[256,512]{1,0:T(8,128)(2,1)S(1)} copy-done((bf16[256,512]{1,0:T(8,128)(2,1)S(1)}, bf16[256,512]{1,0:T(8,128)(2,1)}, u32[]{:S(2)}) %copy-start.2) | copy-done | bytes 262168
  1.0 0.7 %copy-done.6 = s32[256]{0:T(256)S(1)} copy-done((s32[256]{0:T(256)S(1)}, s32[256]{0:T(256)}, u32[]{:S(2)}) %copy-start.6) | copy-done | bytes 1048
  1.6 0.3 gather_rows.1
  1.9 0.5 %collective-permute-start = (bf16[4,32,128]{2,1,0:T(8,128)(2,1)S(1)}, bf16[4,32,128]{2,1,0:T(8,128)(2,1)S(1)}, u32[]{:S(2)}, u32[]{:S(2)}) collective-permute-start(bf16[4,32,128]{2,1,0:T(8,128)(2,1)S(1)} %get-tuple-element.18), channel_id=1, source_target_pairs={{0,1},{1,0},{2,3},{3,2},{4,5},{5,4},{6,7},{7,6},{8,9},{9,8},{10,11... | collective-permute-start | bytes 98312 | tf_op jit(solution)/shard_map/ppermute | solution.py:17
  2.4 2.6 %collective-permute-start.1 = (bf16[4,32,128]{2,1,0:T(8,128)(2,1)S(1)}, bf16[4,32,128]{2,1,0:T(8,128)(2,1)S(1)}, u32[]{:S(2)}, u32[]{:S(2)}) collective-permute-start(bf16[4,32,128]{2,1,0:T(8,128)(2,1)S(1)} %get-tuple-element.19), channel_id=1, source_target_pairs={{0,2},{1,3},{2,0},{3,1},{4,6},{5,7},{6,4},{7,5},{8,10},{9,11},{10,... | collective-permute-start | bytes 98312 | tf_op jit(solution)/shard_map/ppermute | solution.py:17
  5.2 2.8 %collective-permute-start.3 = (bf16[4,32,128]{2,1,0:T(8,128)(2,1)S(1)}, bf16[4,32,128]{2,1,0:T(8,128)(2,1)S(1)}, u32[]{:S(2)}, u32[]{:S(2)}) collective-permute-start(bf16[4,32,128]{2,1,0:T(8,128)(2,1)S(1)} %get-tuple-element.21), channel_id=1, source_target_pairs={{0,4},{1,5},{2,6},{3,7},{4,0},{5,1},{6,2},{7,3},{8,12},{9,13},{10,... | collective-permute-start | bytes 98312 | tf_op jit(solution)/shard_map/ppermute | solution.py:17
  7.9 3.6 %collective-permute-start.5 = (bf16[4,32,128]{2,1,0:T(8,128)(2,1)S(1)}, bf16[4,32,128]{2,1,0:T(8,128)(2,1)S(1)}, u32[]{:S(2)}, u32[]{:S(2)}) collective-permute-start(bf16[4,32,128]{2,1,0:T(8,128)(2,1)S(1)} %get-tuple-element.23), channel_id=1, source_target_pairs={{0,6},{1,7},{2,4},{3,5},{4,2},{5,3},{6,0},{7,1},{8,14},{9,15},{10,... | collective-permute-start | bytes 98312 | tf_op jit(solution)/shard_map/ppermute | solution.py:17
  11.5 0.1 collective-permute-start.6
  11.6 0.6 %collective-permute-done.4.rest_5_ = bf16[4,32,128]{2,1,0:T(8,128)(2,1)S(1)} collective-permute-done((bf16[4,32,128]{2,1,0:T(8,128)(2,1)S(1)}, bf16[4,32,128]{2,1,0:T(8,128)(2,1)S(1)}, u32[]{:S(2)}, u32[]{:S(2)}) %collective-permute-start.4) | collective-permute-done | bytes 32800 | tf_op jit(solution)/shard_map/ppermute | solution.py:17
  12.3 2.0 %collective-permute-done.5.rest_6_ = bf16[4,32,128]{2,1,0:T(8,128)(2,1)S(1)} collective-permute-done((bf16[4,32,128]{2,1,0:T(8,128)(2,1)S(1)}, bf16[4,32,128]{2,1,0:T(8,128)(2,1)S(1)}, u32[]{:S(2)}, u32[]{:S(2)}) %collective-permute-start.5) | collective-permute-done | bytes 32800 | tf_op jit(solution)/shard_map/ppermute | solution.py:17
  14.3 2.3 %collective-permute-done.6.rest_7_ = bf16[4,32,128]{2,1,0:T(8,128)(2,1)S(1)} collective-permute-done((bf16[4,32,128]{2,1,0:T(8,128)(2,1)S(1)}, bf16[4,32,128]{2,1,0:T(8,128)(2,1)S(1)}, u32[]{:S(2)}, u32[]{:S(2)}) %collective-permute-start.6) | collective-permute-done | bytes 32800 | tf_op jit(solution)/shard_map/ppermute | solution.py:17
  16.7 3.4 %copy-done = bf16[2,2048,1024]{2,1,0:T(8,128)(2,1)S(1)} copy-done((bf16[2,2048,1024]{2,1,0:T(8,128)(2,1)S(1)}, bf16[2,2048,1024]{2,1,0:T(8,128)(2,1)}, u32[]{:S(2)}) %copy-start) | copy-done | bytes 8388632
  20.0 1.2 %copy-done.1 = bf16[2,1024,256]{2,1,0:T(8,128)(2,1)S(1)} copy-done((bf16[2,1024,256]{2,1,0:T(8,128)(2,1)S(1)}, bf16[2,1024,256]{2,1,0:T(8,128)(2,1)}, u32[]{:S(2)}) %copy-start.1) | copy-done | bytes 1048600
  21.3 0.7 %copy-done.3 = f32[2,1024]{1,0:T(2,128)S(1)} copy-done((f32[2,1024]{1,0:T(2,128)S(1)}, f32[2,1024]{1,0:T(2,128)}, u32[]{:S(2)}) %copy-start.3) | copy-done | bytes 8216
  22.0 0.7 %copy-done.5 = f32[2,256]{1,0:T(2,128)S(1)} copy-done((f32[2,256]{1,0:T(2,128)S(1)}, f32[2,256]{1,0:T(2,128)}, u32[]{:S(2)}) %copy-start.5) | copy-done | bytes 2072
  22.6 0.7 %copy-done.7 = s32[1,32]{1,0:T(1,128)S(1)} copy-done((s32[1,32]{1,0:T(1,128)S(1)}, s32[1,32]{1,0:T(1,128)}, u32[]{:S(2)}) %copy-start.7) | copy-done | bytes 152
  23.3 2.3 %towers.1 = (bf16[32,128]{1,0:T(8,128)(2,1)S(1)}, bf16[32,128]{1,0:T(8,128)(2,1)S(1)}, bf16[32,128]{1,0:T(8,128)(2,1)S(1)}, bf16[32,128]{1,0:T(8,128)(2,1)S(1)}) custom-call(s32[1,32]{1,0:T(1,128)S(1)} %copy-done.7, bf16[2,2048,1024]{2,1,0:T(8,128)(2,1)S(1)} %copy-done, f32[2,1024]{1,0:T(2,128)S(1)} %copy-done.3, bf16[2,1024,256]{2,1,0:T(8,128)(2,1)S(1)} %copy-done.1, ...), custom_call_target="tpu_custom_call" | custom-call | tf_op jit(solution)/shard_map/towers/pallas_call | solution.py:98
  25.6 1.6 %collective-permute-start.7 = (bf16[32,128]{1,0:T(8,128)(2,1)S(1)}, bf16[32,128]{1,0:T(8,128)(2,1)S(1)}, u32[]{:S(2)}, u32[]{:S(2)}) collective-permute-start(bf16[32,128]{1,0:T(8,128)(2,1)S(1)} %get-tuple-element.26), channel_id=1, source_target_pairs={{0,8},{8,0},{16,24},{24,16},{1,9},{9,1},{17,25},{25,17},{2,10},{10... | collective-permute-start | bytes 24584 | tf_op jit(solution)/shard_map/ppermute | solution.py:17
  27.1 1.5 %collective-permute-start.8 = (bf16[32,128]{1,0:T(8,128)(2,1)S(1)}, bf16[32,128]{1,0:T(8,128)(2,1)S(1)}, u32[]{:S(2)}, u32[]{:S(2)}) collective-permute-start(bf16[32,128]{1,0:T(8,128)(2,1)S(1)} %get-tuple-element.27), channel_id=1, source_target_pairs={{0,16},{8,24},{16,0},{24,8},{1,17},{9,25},{17,1},{25,9},{2,18},{10... | collective-permute-start | bytes 24584 | tf_op jit(solution)/shard_map/ppermute | solution.py:17
  28.7 0.5 %collective-permute-start.9 = (bf16[32,128]{1,0:T(8,128)(2,1)S(1)}, bf16[32,128]{1,0:T(8,128)(2,1)S(1)}, u32[]{:S(2)}, u32[]{:S(2)}) collective-permute-start(bf16[32,128]{1,0:T(8,128)(2,1)S(1)} %get-tuple-element.28), channel_id=1, source_target_pairs={{0,24},{8,16},{16,8},{24,0},{1,25},{9,17},{17,9},{25,1},{2,26},{10... | collective-permute-start | bytes 24584 | tf_op jit(solution)/shard_map/ppermute | solution.py:17
  29.1 0.2 collective-permute-done.7.rest_1_
  29.3 1.5 %collective-permute-done.8.rest_2_ = bf16[32,128]{1,0:T(8,128)(2,1)S(1)} collective-permute-done((bf16[32,128]{1,0:T(8,128)(2,1)S(1)}, bf16[32,128]{1,0:T(8,128)(2,1)S(1)}, u32[]{:S(2)}, u32[]{:S(2)}) %collective-permute-start.8) | collective-permute-done | bytes 8224 | tf_op jit(solution)/shard_map/ppermute | solution.py:17
  30.8 2.4 %collective-permute-done.9.rest_3_ = bf16[32,128]{1,0:T(8,128)(2,1)S(1)} collective-permute-done((bf16[32,128]{1,0:T(8,128)(2,1)S(1)}, bf16[32,128]{1,0:T(8,128)(2,1)S(1)}, u32[]{:S(2)}, u32[]{:S(2)}) %collective-permute-start.9) | collective-permute-done | bytes 8224 | tf_op jit(solution)/shard_map/ppermute | solution.py:17
  33.2 0.9 %interact.1 = bf16[8,16,128]{2,1,0:T(8,128)(2,1)} custom-call(bf16[16,128]{1,0:T(8,128)(2,1)S(1)} %copy-done.4, bf16[32,128]{1,0:T(8,128)(2,1)S(1)} %get-tuple-element.25.rest_0_, bf16[32,128]{1,0:T(8,128)(2,1)S(1)} %collective-permute-done.7.rest_1_, bf16[32,128]{1,0:T(8,128)(2,1)S(1)} %collective-permute-done.8.rest_2_, ...), custom_call_target="tpu_custom_call" | custom-call | tf_op jit(solution)/shard_map/interact/pallas_call | solution.py:156
  (15 shorter events, 0.1 us)
Async XLA Ops:
  0.0 0.9 %copy-start.2 = (bf16[256,512]{1,0:T(8,128)(2,1)S(1)}, bf16[256,512]{1,0:T(8,128)(2,1)}, u32[]{:S(2)}) copy-start(bf16[256,512]{1,0:T(8,128)(2,1)} %emb_ref.1) | copy-start | bytes 786436
  1.0 0.7 %copy-start.6 = (s32[256]{0:T(256)S(1)}, s32[256]{0:T(256)}, u32[]{:S(2)}) copy-start(s32[256]{0:T(256)} %owner_ref.1) | copy-start | bytes 3076
  1.6 31.6 %copy-start.4 = (bf16[16,128]{1,0:T(8,128)(2,1)S(1)}, bf16[16,128]{1,0:T(8,128)(2,1)}, u32[]{:S(2)}) copy-start(bf16[16,128]{1,0:T(8,128)(2,1)} %proj_ref.1) | copy-start | bytes 12292
  1.9 6.0 %collective-permute-start = (bf16[4,32,128]{2,1,0:T(8,128)(2,1)S(1)}, bf16[4,32,128]{2,1,0:T(8,128)(2,1)S(1)}, u32[]{:S(2)}, u32[]{:S(2)}) collective-permute-start(bf16[4,32,128]{2,1,0:T(8,128)(2,1)S(1)} %get-tuple-element.18), channel_id=1, source_target_pairs={{0,1},{1,0},{2,3},{3,2},{4,5},{5,4},{6,7},{7,6},{8,9},{9,8},{10,11... | collective-permute-start | bytes 98312 | tf_op jit(solution)/shard_map/ppermute | solution.py:17
  2.4 9.1 %collective-permute-start.1 = (bf16[4,32,128]{2,1,0:T(8,128)(2,1)S(1)}, bf16[4,32,128]{2,1,0:T(8,128)(2,1)S(1)}, u32[]{:S(2)}, u32[]{:S(2)}) collective-permute-start(bf16[4,32,128]{2,1,0:T(8,128)(2,1)S(1)} %get-tuple-element.19), channel_id=1, source_target_pairs={{0,2},{1,3},{2,0},{3,1},{4,6},{5,7},{6,4},{7,5},{8,10},{9,11},{10,... | collective-permute-start | bytes 98312 | tf_op jit(solution)/shard_map/ppermute | solution.py:17
  5.1 6.6 %collective-permute-start.2 = (bf16[4,32,128]{2,1,0:T(8,128)(2,1)S(1)}, bf16[4,32,128]{2,1,0:T(8,128)(2,1)S(1)}, u32[]{:S(2)}, u32[]{:S(2)}) collective-permute-start(bf16[4,32,128]{2,1,0:T(8,128)(2,1)S(1)} %get-tuple-element.20), channel_id=1, source_target_pairs={{0,3},{1,2},{2,1},{3,0},{4,7},{5,6},{6,5},{7,4},{8,11},{9,10},{10,... | collective-permute-start | bytes 98312 | tf_op jit(solution)/shard_map/ppermute | solution.py:17
  5.2 6.5 %collective-permute-start.3 = (bf16[4,32,128]{2,1,0:T(8,128)(2,1)S(1)}, bf16[4,32,128]{2,1,0:T(8,128)(2,1)S(1)}, u32[]{:S(2)}, u32[]{:S(2)}) collective-permute-start(bf16[4,32,128]{2,1,0:T(8,128)(2,1)S(1)} %get-tuple-element.21), channel_id=1, source_target_pairs={{0,4},{1,5},{2,6},{3,7},{4,0},{5,1},{6,2},{7,3},{8,12},{9,13},{10,... | collective-permute-start | bytes 98312 | tf_op jit(solution)/shard_map/ppermute | solution.py:17
  7.9 4.4 %collective-permute-start.4 = (bf16[4,32,128]{2,1,0:T(8,128)(2,1)S(1)}, bf16[4,32,128]{2,1,0:T(8,128)(2,1)S(1)}, u32[]{:S(2)}, u32[]{:S(2)}) collective-permute-start(bf16[4,32,128]{2,1,0:T(8,128)(2,1)S(1)} %get-tuple-element.22), channel_id=1, source_target_pairs={{0,5},{1,4},{2,7},{3,6},{4,1},{5,0},{6,3},{7,2},{8,13},{9,12},{10,... | collective-permute-start | bytes 98312 | tf_op jit(solution)/shard_map/ppermute | solution.py:17
  7.9 6.4 %collective-permute-start.5 = (bf16[4,32,128]{2,1,0:T(8,128)(2,1)S(1)}, bf16[4,32,128]{2,1,0:T(8,128)(2,1)S(1)}, u32[]{:S(2)}, u32[]{:S(2)}) collective-permute-start(bf16[4,32,128]{2,1,0:T(8,128)(2,1)S(1)} %get-tuple-element.23), channel_id=1, source_target_pairs={{0,6},{1,7},{2,4},{3,5},{4,2},{5,3},{6,0},{7,1},{8,14},{9,15},{10,... | collective-permute-start | bytes 98312 | tf_op jit(solution)/shard_map/ppermute | solution.py:17
  11.5 5.1 %collective-permute-start.6 = (bf16[4,32,128]{2,1,0:T(8,128)(2,1)S(1)}, bf16[4,32,128]{2,1,0:T(8,128)(2,1)S(1)}, u32[]{:S(2)}, u32[]{:S(2)}) collective-permute-start(bf16[4,32,128]{2,1,0:T(8,128)(2,1)S(1)} %get-tuple-element.24), channel_id=1, source_target_pairs={{0,7},{1,6},{2,5},{3,4},{4,3},{5,2},{6,1},{7,0},{8,15},{9,14},{10,... | collective-permute-start | bytes 98312 | tf_op jit(solution)/shard_map/ppermute | solution.py:17
  16.7 3.4 %copy-start = (bf16[2,2048,1024]{2,1,0:T(8,128)(2,1)S(1)}, bf16[2,2048,1024]{2,1,0:T(8,128)(2,1)}, u32[]{:S(2)}) copy-start(bf16[2,2048,1024]{2,1,0:T(8,128)(2,1)} %w1_ref.1) | copy-start | bytes 25165828
  20.0 1.2 %copy-start.1 = (bf16[2,1024,256]{2,1,0:T(8,128)(2,1)S(1)}, bf16[2,1024,256]{2,1,0:T(8,128)(2,1)}, u32[]{:S(2)}) copy-start(bf16[2,1024,256]{2,1,0:T(8,128)(2,1)} %w2_ref.1) | copy-start | bytes 3145732
  21.3 0.7 %copy-start.3 = (f32[2,1024]{1,0:T(2,128)S(1)}, f32[2,1024]{1,0:T(2,128)}, u32[]{:S(2)}) copy-start(f32[2,1024]{1,0:T(2,128)} %b1_ref.1) | copy-start | bytes 24580
  22.0 0.7 %copy-start.5 = (f32[2,256]{1,0:T(2,128)S(1)}, f32[2,256]{1,0:T(2,128)}, u32[]{:S(2)}) copy-start(f32[2,256]{1,0:T(2,128)} %b2_ref.1) | copy-start | bytes 6148
  22.6 0.7 %copy-start.7 = (s32[1,32]{1,0:T(1,128)S(1)}, s32[1,32]{1,0:T(1,128)}, u32[]{:S(2)}) copy-start(s32[1,32]{1,0:T(1,128)} %assign_ref.1) | copy-start | bytes 388
  25.6 3.7 %collective-permute-start.7 = (bf16[32,128]{1,0:T(8,128)(2,1)S(1)}, bf16[32,128]{1,0:T(8,128)(2,1)S(1)}, u32[]{:S(2)}, u32[]{:S(2)}) collective-permute-start(bf16[32,128]{1,0:T(8,128)(2,1)S(1)} %get-tuple-element.26), channel_id=1, source_target_pairs={{0,8},{8,0},{16,24},{24,16},{1,9},{9,1},{17,25},{25,17},{2,10},{10... | collective-permute-start | bytes 24584 | tf_op jit(solution)/shard_map/ppermute | solution.py:17
  27.1 3.7 %collective-permute-start.8 = (bf16[32,128]{1,0:T(8,128)(2,1)S(1)}, bf16[32,128]{1,0:T(8,128)(2,1)S(1)}, u32[]{:S(2)}, u32[]{:S(2)}) collective-permute-start(bf16[32,128]{1,0:T(8,128)(2,1)S(1)} %get-tuple-element.27), channel_id=1, source_target_pairs={{0,16},{8,24},{16,0},{24,8},{1,17},{9,25},{17,1},{25,9},{2,18},{10... | collective-permute-start | bytes 24584 | tf_op jit(solution)/shard_map/ppermute | solution.py:17
  28.7 4.5 %collective-permute-start.9 = (bf16[32,128]{1,0:T(8,128)(2,1)S(1)}, bf16[32,128]{1,0:T(8,128)(2,1)S(1)}, u32[]{:S(2)}, u32[]{:S(2)}) collective-permute-start(bf16[32,128]{1,0:T(8,128)(2,1)S(1)} %get-tuple-element.28), channel_id=1, source_target_pairs={{0,24},{8,16},{16,8},{24,0},{1,25},{9,17},{17,9},{25,1},{2,26},{10... | collective-permute-start | bytes 24584 | tf_op jit(solution)/shard_map/ppermute | solution.py:17

commit v2 on v1

--- a/solution.py
+++ b/solution.py
@@ -11,50 +11,76 @@
 FEW_SAMPLES = 1024
 
 
-def swap(block, axis, size, offset):
-    if offset == 0:
-        return block
-    return lax.ppermute(block, axis, [(i, i ^ offset) for i in range(size)])
-
-
-def gather_kernel(towers, intra, owner_ref, emb_ref, *rest):
-    outs, acc_ref = rest[:intra], rest[intra]
+def offsets(size):
+    return range(size - 1, -1, -1)
+
+
+def exchange(blocks, axis, size):
+    return [
+        lax.ppermute(block, axis, [(i, i ^ o) for i in range(size)]) if o else block
+        for block, o in zip(blocks, offsets(size))
+    ]
+
+
+def gather_kernel(towers, intra, count, owner_hbm, emb_hbm, *rest):
+    small, rest = rest[:count], rest[count:]
+    outs, rest = rest[:intra], rest[intra:]
+    copies, (owner_ref, emb_ref, acc_ref, sems) = rest[:count], rest[count:]
+    pairs = [(owner_hbm, owner_ref), (emb_hbm, emb_ref), *zip(small, copies)]
+    loads = [pltpu.make_async_copy(a, b, sems.at[i]) for i, (a, b) in enumerate(pairs)]
+    for load in loads:
+        load.start()
     samples, width = emb_ref.shape
     per = samples // (towers * intra)
     me = lax.axis_index("intra")
+    loads[0].wait()
     owner = jnp.broadcast_to(owner_ref[...].reshape(1, samples), (samples, samples))
     picks = lax.broadcasted_iota(jnp.int32, (samples, samples), 0) == owner
     picks = jnp.where(picks, 1.0, 0.0).astype(jnp.bfloat16)
+    loads[1].wait()
     acc_ref[...] = lax.dot_general(
         picks, emb_ref[...], (((0,), (0,)), ((), ())), preferred_element_type=jnp.float32
     )
-    for o, out in enumerate(outs):
+    for o, out in zip(offsets(intra), outs):
         block = me ^ o
         starts = [pl.multiple_of((t * intra + block) * per, per) for t in range(towers)]
         for f in range(width // EDIM):
             columns = slice(f * EDIM, (f + 1) * EDIM)
             rows = [acc_ref[pl.ds(start, per), columns] for start in starts]
             out[f] = jnp.concatenate(rows, axis=0).astype(out.dtype)
-
-
-def gather_blocks(owner, embeddings, towers, intra):
+    for load in loads[2:]:
+        load.wait()
+
+
+def gather_blocks(owner, embeddings, small, towers, intra, ahead):
     samples, width = embeddings.shape
     rows, held = samples // intra, width // EDIM
-    shape = jax.ShapeDtypeStruct((held, rows, EDIM), embeddings.dtype)
     if samples <= FEW_SAMPLES:
-        return pl.pallas_call(
-            functools.partial(gather_kernel, towers, intra),
-            out_shape=[shape] * intra,
-            in_specs=[pl.BlockSpec(memory_space=pltpu.VMEM)] * 2,
-            out_specs=[pl.BlockSpec(memory_space=pltpu.VMEM)] * intra,
-            scratch_shapes=[pltpu.VMEM((samples, width), jnp.float32)],
+        count = len(small)
+        shape = pltpu.VMEM((held, rows, EDIM), embeddings.dtype)
+        given = [pltpu.with_memory_space_constraint(a, pltpu.HBM) for a in (owner, embeddings, *small)]
+        spaces = [pltpu.SMEM if jnp.issubdtype(a.dtype, jnp.integer) else pltpu.VMEM for a in small]
+        results = pl.pallas_call(
+            functools.partial(gather_kernel, towers, intra, count),
+            out_shape=[shape] * intra + [space(a.shape, a.dtype) for space, a in zip(spaces, small)],
+            in_specs=[pl.BlockSpec(memory_space=pltpu.HBM)] * len(given),
+            out_specs=[pl.BlockSpec(memory_space=pltpu.VMEM)] * intra
+            + [pl.BlockSpec(memory_space=space) for space in spaces],
+            scratch_shapes=[
+                pltpu.VMEM(owner.shape, owner.dtype),
+                pltpu.VMEM(embeddings.shape, embeddings.dtype),
+                pltpu.VMEM((samples, width), jnp.float32),
+                pltpu.SemaphoreType.DMA((len(given),)),
+            ],
             compiler_params=pltpu.CompilerParams(vmem_limit_bytes=8 << 20),
+            cost_estimate=pl.CostEstimate(flops=ahead, bytes_accessed=0, transcendentals=0),
             name="gather_rows",
-        )(owner, embeddings)
+        )(*given)
+        return results[:intra], results[intra:]
     order = owner.reshape(towers, intra, -1).transpose(1, 0, 2).reshape(-1)
     blocks = jnp.take(embeddings, order, axis=0).reshape(intra, rows, held, EDIM).transpose(0, 2, 1, 3)
     me = lax.axis_index("intra")
-    return [lax.dynamic_index_in_dim(blocks, me ^ o, keepdims=False) for o in range(intra)]
+    return [lax.dynamic_index_in_dim(blocks, me ^ o, keepdims=False) for o in offsets(intra)], small
 
 
 def tower_kernel(towers, intra, assign_ref, w1_ref, b1_ref, w2_ref, b2_ref, *rest):
@@ -66,7 +92,7 @@
     per = rows // towers
     slots = depth // EDIM
     me = lax.axis_index("intra")
-    for o, block in enumerate(blocks):
+    for o, block in zip(offsets(intra), blocks):
         pool_ref[pl.ds((me ^ o) * held, held)] = block[...]
     for k in range(count):
         for j in range(slots):
@@ -77,7 +103,7 @@
         result = jnp.dot(hidden, w2_ref[k], preferred_element_type=jnp.float32)
         y_ref[k] = jnp.maximum(result + b2_ref[k : k + 1, :], 0.0)
     place = lax.axis_index("tower")
-    for o, out in enumerate(outs):
+    for o, out in zip(offsets(towers), outs):
         start = pl.multiple_of((place ^ o) * per, per)
         pieces = [
             y_ref[k, pl.ds(start, per), v * EDIM : (v + 1) * EDIM]
@@ -116,7 +142,7 @@
     per, count, _ = out.shape
     local = blocks[0].shape[0]
     place = lax.axis_index("tower")
-    for o, block in enumerate(blocks):
+    for o, block in zip(offsets(towers), blocks):
         start = pl.multiple_of((place ^ o) * local, local)
         all_ref[pl.ds(start, local), :] = block[...].astype(jnp.float32)
     group = max(1, min(per, 128 // count))
@@ -175,12 +201,15 @@
     proj_weight,
 ):
     towers, intra = lax.axis_size("tower"), lax.axis_size("intra")
-    blocks = gather_blocks(sample_owner, embeddings, towers, intra)
-    blocks = [swap(block, "intra", intra, o) for o, block in enumerate(blocks)]
+    small = (feature_assign, first_bias, tower_bias, proj_weight)
+    ahead = 10_000 * (first_weight.size + tower_weight.size)
+    blocks, small = gather_blocks(sample_owner, embeddings, small, towers, intra, ahead)
+    feature_assign, first_bias, tower_bias, proj_weight = small
+    blocks = exchange(blocks, "intra", intra)
     vectors = run_towers(
         feature_assign, first_weight, first_bias, tower_weight, tower_bias, blocks, towers
     )
-    vectors = [swap(block, "tower", towers, o) for o, block in enumerate(vectors)]
+    vectors = exchange(vectors, "tower", towers)
     return interact(proj_weight, vectors)
 
 

time: 34.5 us -> 23.9 us (0.69)
  local copies, waits for them, and re-layouts: 8.27 us -> 0.01 us
  waiting for transfers between devices: 9.09 us -> 6.46 us
  Pallas kernels: 3.51 us -> 4.13 us
    unnamed x16 -> x4, local copies, waits for them, and re-layouts: 8.27 us -> 0.01 us
    ppermute x10, waiting for transfers between devices: 9.09 us -> 6.46 us  [exchange(): lax.ppermute(block, axis, [(i, i ^ o) for i in range(size)])]
    pallas_call x1, Pallas kernels: 0.28 us -> 1.46 us  [gather_blocks(): pl.pallas_call(functools.partial(gather_kernel, towers, intra, count), ou...]
    pallas_call x1, Pallas kernels: 2.29 us -> 1.72 us  [run_towers(): pl.pallas_call(functools.partial(tower_kernel, towers, intra), out_shape=...]
where the time goes in v2:
time: 23.9 us; the launch traced here: 23.8 us
  starting transfers between devices  13.1 us (55%)
  waiting for transfers between devices  6.46 us (27%)
  Pallas kernels  4.13 us (17%)
    ppermute x10, starting transfers between devices, exchange(): lax.ppermute(block, axis, [(i, i ^ o) for i in range(size)])  13.1 us
    ppermute x10, waiting for transfers between devices, exchange(): lax.ppermute(block, axis, [(i, i ^ o) for i in range(size)])  6.46 us
    pallas_call x1, Pallas kernels, run_towers(): pl.pallas_call(functools.partial(tower_kernel, towers, intra), out_shape=...  1.72 us
    pallas_call x1, Pallas kernels, gather_blocks(): pl.pallas_call(functools.partial(gather_kernel, towers, intra, count), ou...  1.46 us
    pallas_call x1, Pallas kernels, interact(): pl.pallas_call(functools.partial(interact_kernel, towers), out_shape=jax....  0.94 us
  transfers between devices with their start and end apart: 10, of which 6 were waited for; matrix products, arithmetic and copies ran while one was open for 0% of the time, Pallas kernels for 0%

profile of v2, /device:TPU:0, one launch (start us, length us, event | category | flops | bytes accessed | tf_op | source)
XLA Modules:
  0.0 23.8 jit_solution(15066824751866239364)
XLA Ops:
  0.0 1.5 %gather_rows.1 = (bf16[4,32,128]{2,1,0:T(8,128)(2,1)S(1)}, bf16[4,32,128]{2,1,0:T(8,128)(2,1)S(1)}, bf16[4,32,128]{2,1,0:T(8,128)(2,1)S(1)}, bf16[4,32,128]{2,1,...) custom-call(s32[256]{0:T(256)} %owner_hbm.1, ...), custom_call_target="tpu_custom_call" | custom-call | flops 47185920000 | tf_op jit(solution)/shard_map/gather_rows/pallas_call | solution.py:63
  1.5 4.5 %collective-permute-start = (bf16[4,32,128]{2,1,0:T(8,128)(2,1)S(1)}, bf16[4,32,128]{2,1,0:T(8,128)(2,1)S(1)}, u32[]{:S(2)}, u32[]{:S(2)}) collective-permute-start(bf16[4,32,128]{2,1,0:T(8,128)(2,1)S(1)} %get-tuple-element.25), channel_id=1, source_target_pairs={{0,7},{1,6},{2,5},{3,4},{4,3},{5,2},{6,1},{7,0},{8,15},{9,14},{10,... | collective-permute-start | bytes 98312 | tf_op jit(solution)/shard_map/ppermute | solution.py:20
  6.0 0.6 %collective-permute-start.1 = (bf16[4,32,128]{2,1,0:T(8,128)(2,1)S(1)}, bf16[4,32,128]{2,1,0:T(8,128)(2,1)S(1)}, u32[]{:S(2)}, u32[]{:S(2)}) collective-permute-start(bf16[4,32,128]{2,1,0:T(8,128)(2,1)S(1)} %get-tuple-element.26), channel_id=1, source_target_pairs={{0,6},{1,7},{2,4},{3,5},{4,2},{5,3},{6,0},{7,1},{8,14},{9,15},{10,... | collective-permute-start | bytes 98312 | tf_op jit(solution)/shard_map/ppermute | solution.py:20
  6.7 0.4 %collective-permute-start.2 = (bf16[4,32,128]{2,1,0:T(8,128)(2,1)S(1)}, bf16[4,32,128]{2,1,0:T(8,128)(2,1)S(1)}, u32[]{:S(2)}, u32[]{:S(2)}) collective-permute-start(bf16[4,32,128]{2,1,0:T(8,128)(2,1)S(1)} %get-tuple-element.27), channel_id=1, source_target_pairs={{0,5},{1,4},{2,7},{3,6},{4,1},{5,0},{6,3},{7,2},{8,13},{9,12},{10,... | collective-permute-start | bytes 98312 | tf_op jit(solution)/shard_map/ppermute | solution.py:20
  7.0 2.2 %collective-permute-start.3 = (bf16[4,32,128]{2,1,0:T(8,128)(2,1)S(1)}, bf16[4,32,128]{2,1,0:T(8,128)(2,1)S(1)}, u32[]{:S(2)}, u32[]{:S(2)}) collective-permute-start(bf16[4,32,128]{2,1,0:T(8,128)(2,1)S(1)} %get-tuple-element.28), channel_id=1, source_target_pairs={{0,4},{1,5},{2,6},{3,7},{4,0},{5,1},{6,2},{7,3},{8,12},{9,13},{10,... | collective-permute-start | bytes 98312 | tf_op jit(solution)/shard_map/ppermute | solution.py:20
  9.2 1.0 %collective-permute-start.4 = (bf16[4,32,128]{2,1,0:T(8,128)(2,1)S(1)}, bf16[4,32,128]{2,1,0:T(8,128)(2,1)S(1)}, u32[]{:S(2)}, u32[]{:S(2)}) collective-permute-start(bf16[4,32,128]{2,1,0:T(8,128)(2,1)S(1)} %get-tuple-element.29), channel_id=1, source_target_pairs={{0,3},{1,2},{2,1},{3,0},{4,7},{5,6},{6,5},{7,4},{8,11},{9,10},{10,... | collective-permute-start | bytes 98312 | tf_op jit(solution)/shard_map/ppermute | solution.py:20
  10.2 0.0 collective-permute-done.rest_0_
  10.2 0.9 %collective-permute-start.5 = (bf16[4,32,128]{2,1,0:T(8,128)(2,1)S(1)}, bf16[4,32,128]{2,1,0:T(8,128)(2,1)S(1)}, u32[]{:S(2)}, u32[]{:S(2)}) collective-permute-start(bf16[4,32,128]{2,1,0:T(8,128)(2,1)S(1)} %get-tuple-element.30), channel_id=1, source_target_pairs={{0,2},{1,3},{2,0},{3,1},{4,6},{5,7},{6,4},{7,5},{8,10},{9,11},{10,... | collective-permute-start | bytes 98312 | tf_op jit(solution)/shard_map/ppermute | solution.py:20
  11.1 1.1 %collective-permute-done.1.rest_1_ = bf16[4,32,128]{2,1,0:T(8,128)(2,1)S(1)} collective-permute-done((bf16[4,32,128]{2,1,0:T(8,128)(2,1)S(1)}, bf16[4,32,128]{2,1,0:T(8,128)(2,1)S(1)}, u32[]{:S(2)}, u32[]{:S(2)}) %collective-permute-start.1) | collective-permute-done | bytes 32800 | tf_op jit(solution)/shard_map/ppermute | solution.py:20
  12.2 0.0 collective-permute-start.6
  12.2 0.0 collective-permute-done.2.rest_2_
  12.2 1.3 %collective-permute-done.3.rest_3_ = bf16[4,32,128]{2,1,0:T(8,128)(2,1)S(1)} collective-permute-done((bf16[4,32,128]{2,1,0:T(8,128)(2,1)S(1)}, bf16[4,32,128]{2,1,0:T(8,128)(2,1)S(1)}, u32[]{:S(2)}, u32[]{:S(2)}) %collective-permute-start.3) | collective-permute-done | bytes 32800 | tf_op jit(solution)/shard_map/ppermute | solution.py:20
  13.5 0.0 collective-permute-done.4.rest_4_
  13.5 0.9 %collective-permute-done.5.rest_5_ = bf16[4,32,128]{2,1,0:T(8,128)(2,1)S(1)} collective-permute-done((bf16[4,32,128]{2,1,0:T(8,128)(2,1)S(1)}, bf16[4,32,128]{2,1,0:T(8,128)(2,1)S(1)}, u32[]{:S(2)}, u32[]{:S(2)}) %collective-permute-start.5) | collective-permute-done | bytes 32800 | tf_op jit(solution)/shard_map/ppermute | solution.py:20
  14.4 0.0 collective-permute-done.6.rest_6_
  14.4 0.0 copy-done.1
  14.4 1.7 %towers.1 = (bf16[32,128]{1,0:T(8,128)(2,1)S(1)}, bf16[32,128]{1,0:T(8,128)(2,1)S(1)}, bf16[32,128]{1,0:T(8,128)(2,1)S(1)}, bf16[32,128]{1,0:T(8,128)(2,1)S(1)}) custom-call(s32[1,32]{1,0:T(1,128)S(4)} %get-tuple-element.22.assign_ref, bf16[2,2048,1024]{2,1,0:T(8,128)(2,1)S(1)} %copy-done, f32[2,1024]{1,0:T(2,128)S(1)} %get-tuple-element.23.b1_ref, ...), custom_call_target="tpu_custom_call" | custom-call | tf_op jit(solution)/shard_map/towers/pallas_call | solution.py:124
  16.1 2.5 %collective-permute-start.7 = (bf16[32,128]{1,0:T(8,128)(2,1)S(1)}, bf16[32,128]{1,0:T(8,128)(2,1)S(1)}, u32[]{:S(2)}, u32[]{:S(2)}) collective-permute-start(bf16[32,128]{1,0:T(8,128)(2,1)S(1)} %get-tuple-element.33), channel_id=1, source_target_pairs={{0,24},{8,16},{16,8},{24,0},{1,25},{9,17},{17,9},{25,1},{2,26},{10... | collective-permute-start | bytes 24584 | tf_op jit(solution)/shard_map/ppermute | solution.py:20
  18.7 0.5 %collective-permute-start.8 = (bf16[32,128]{1,0:T(8,128)(2,1)S(1)}, bf16[32,128]{1,0:T(8,128)(2,1)S(1)}, u32[]{:S(2)}, u32[]{:S(2)}) collective-permute-start(bf16[32,128]{1,0:T(8,128)(2,1)S(1)} %get-tuple-element.34), channel_id=1, source_target_pairs={{0,16},{8,24},{16,0},{24,8},{1,17},{9,25},{17,1},{25,9},{2,18},{10... | collective-permute-start | bytes 24584 | tf_op jit(solution)/shard_map/ppermute | solution.py:20
  19.2 0.5 %collective-permute-start.9 = (bf16[32,128]{1,0:T(8,128)(2,1)S(1)}, bf16[32,128]{1,0:T(8,128)(2,1)S(1)}, u32[]{:S(2)}, u32[]{:S(2)}) collective-permute-start(bf16[32,128]{1,0:T(8,128)(2,1)S(1)} %get-tuple-element.35), channel_id=1, source_target_pairs={{0,8},{8,0},{16,24},{24,16},{1,9},{9,1},{17,25},{25,17},{2,10},{10... | collective-permute-start | bytes 24584 | tf_op jit(solution)/shard_map/ppermute | solution.py:20
  19.7 1.1 %collective-permute-done.7.rest_0_ = bf16[32,128]{1,0:T(8,128)(2,1)S(1)} collective-permute-done((bf16[32,128]{1,0:T(8,128)(2,1)S(1)}, bf16[32,128]{1,0:T(8,128)(2,1)S(1)}, u32[]{:S(2)}, u32[]{:S(2)}) %collective-permute-start.7) | collective-permute-done | bytes 8224 | tf_op jit(solution)/shard_map/ppermute | solution.py:20
  20.8 1.5 %collective-permute-done.8.rest_1_ = bf16[32,128]{1,0:T(8,128)(2,1)S(1)} collective-permute-done((bf16[32,128]{1,0:T(8,128)(2,1)S(1)}, bf16[32,128]{1,0:T(8,128)(2,1)S(1)}, u32[]{:S(2)}, u32[]{:S(2)}) %collective-permute-start.8) | collective-permute-done | bytes 8224 | tf_op jit(solution)/shard_map/ppermute | solution.py:20
  22.3 0.5 %collective-permute-done.9.rest_2_ = bf16[32,128]{1,0:T(8,128)(2,1)S(1)} collective-permute-done((bf16[32,128]{1,0:T(8,128)(2,1)S(1)}, bf16[32,128]{1,0:T(8,128)(2,1)S(1)}, u32[]{:S(2)}, u32[]{:S(2)}) %collective-permute-start.9) | collective-permute-done | bytes 8224 | tf_op jit(solution)/shard_map/ppermute | solution.py:20
  22.8 0.9 %interact.1 = bf16[8,16,128]{2,1,0:T(8,128)(2,1)} custom-call(bf16[16,128]{1,0:T(8,128)(2,1)S(1)} %get-tuple-element.21.proj_ref, bf16[32,128]{1,0:T(8,128)(2,1)S(1)} %collective-permute-done.7.rest_0_, bf16[32,128]{1,0:T(8,128)(2,1)S(1)} %collective-permute-done.8.rest_1_, bf16[32,128]{1,0:T(8,128)(2,1)S(1)} %collective-permute-done.9.rest_2_, ...), custom_call_target="tpu_custom_call" | custom-call | tf_op jit(solution)/shard_map/interact/pallas_call | solution.py:182
  (3 shorter events, 0.0 us)
Async XLA Ops:
  0.0 14.4 %copy-start.1 = (bf16[2,1024,256]{2,1,0:T(8,128)(2,1)S(1)}, bf16[2,1024,256]{2,1,0:T(8,128)(2,1)}, u32[]{:S(2)}) copy-start(bf16[2,1024,256]{2,1,0:T(8,128)(2,1)} %w2_ref.1) | copy-start | bytes 3145732
  0.0 14.4 %copy-start = (bf16[2,2048,1024]{2,1,0:T(8,128)(2,1)S(1)}, bf16[2,2048,1024]{2,1,0:T(8,128)(2,1)}, u32[]{:S(2)}) copy-start(bf16[2,2048,1024]{2,1,0:T(8,128)(2,1)} %w1_ref.1) | copy-start | bytes 25165828
  1.5 8.7 %collective-permute-start = (bf16[4,32,128]{2,1,0:T(8,128)(2,1)S(1)}, bf16[4,32,128]{2,1,0:T(8,128)(2,1)S(1)}, u32[]{:S(2)}, u32[]{:S(2)}) collective-permute-start(bf16[4,32,128]{2,1,0:T(8,128)(2,1)S(1)} %get-tuple-element.25), channel_id=1, source_target_pairs={{0,7},{1,6},{2,5},{3,4},{4,3},{5,2},{6,1},{7,0},{8,15},{9,14},{10,... | collective-permute-start | bytes 98312 | tf_op jit(solution)/shard_map/ppermute | solution.py:20
  6.0 6.2 %collective-permute-start.1 = (bf16[4,32,128]{2,1,0:T(8,128)(2,1)S(1)}, bf16[4,32,128]{2,1,0:T(8,128)(2,1)S(1)}, u32[]{:S(2)}, u32[]{:S(2)}) collective-permute-start(bf16[4,32,128]{2,1,0:T(8,128)(2,1)S(1)} %get-tuple-element.26), channel_id=1, source_target_pairs={{0,6},{1,7},{2,4},{3,5},{4,2},{5,3},{6,0},{7,1},{8,14},{9,15},{10,... | collective-permute-start | bytes 98312 | tf_op jit(solution)/shard_map/ppermute | solution.py:20
  6.7 5.5 %collective-permute-start.2 = (bf16[4,32,128]{2,1,0:T(8,128)(2,1)S(1)}, bf16[4,32,128]{2,1,0:T(8,128)(2,1)S(1)}, u32[]{:S(2)}, u32[]{:S(2)}) collective-permute-start(bf16[4,32,128]{2,1,0:T(8,128)(2,1)S(1)} %get-tuple-element.27), channel_id=1, source_target_pairs={{0,5},{1,4},{2,7},{3,6},{4,1},{5,0},{6,3},{7,2},{8,13},{9,12},{10,... | collective-permute-start | bytes 98312 | tf_op jit(solution)/shard_map/ppermute | solution.py:20
  7.0 6.4 %collective-permute-start.3 = (bf16[4,32,128]{2,1,0:T(8,128)(2,1)S(1)}, bf16[4,32,128]{2,1,0:T(8,128)(2,1)S(1)}, u32[]{:S(2)}, u32[]{:S(2)}) collective-permute-start(bf16[4,32,128]{2,1,0:T(8,128)(2,1)S(1)} %get-tuple-element.28), channel_id=1, source_target_pairs={{0,4},{1,5},{2,6},{3,7},{4,0},{5,1},{6,2},{7,3},{8,12},{9,13},{10,... | collective-permute-start | bytes 98312 | tf_op jit(solution)/shard_map/ppermute | solution.py:20
  9.2 4.2 %collective-permute-start.4 = (bf16[4,32,128]{2,1,0:T(8,128)(2,1)S(1)}, bf16[4,32,128]{2,1,0:T(8,128)(2,1)S(1)}, u32[]{:S(2)}, u32[]{:S(2)}) collective-permute-start(bf16[4,32,128]{2,1,0:T(8,128)(2,1)S(1)} %get-tuple-element.29), channel_id=1, source_target_pairs={{0,3},{1,2},{2,1},{3,0},{4,7},{5,6},{6,5},{7,4},{8,11},{9,10},{10,... | collective-permute-start | bytes 98312 | tf_op jit(solution)/shard_map/ppermute | solution.py:20
  10.2 4.2 %collective-permute-start.5 = (bf16[4,32,128]{2,1,0:T(8,128)(2,1)S(1)}, bf16[4,32,128]{2,1,0:T(8,128)(2,1)S(1)}, u32[]{:S(2)}, u32[]{:S(2)}) collective-permute-start(bf16[4,32,128]{2,1,0:T(8,128)(2,1)S(1)} %get-tuple-element.30), channel_id=1, source_target_pairs={{0,2},{1,3},{2,0},{3,1},{4,6},{5,7},{6,4},{7,5},{8,10},{9,11},{10,... | collective-permute-start | bytes 98312 | tf_op jit(solution)/shard_map/ppermute | solution.py:20
  12.2 2.2 %collective-permute-start.6 = (bf16[4,32,128]{2,1,0:T(8,128)(2,1)S(1)}, bf16[4,32,128]{2,1,0:T(8,128)(2,1)S(1)}, u32[]{:S(2)}, u32[]{:S(2)}) collective-permute-start(bf16[4,32,128]{2,1,0:T(8,128)(2,1)S(1)} %get-tuple-element.31), channel_id=1, source_target_pairs={{0,1},{1,0},{2,3},{3,2},{4,5},{5,4},{6,7},{7,6},{8,9},{9,8},{10,11... | collective-permute-start | bytes 98312 | tf_op jit(solution)/shard_map/ppermute | solution.py:20
  16.1 4.6 %collective-permute-start.7 = (bf16[32,128]{1,0:T(8,128)(2,1)S(1)}, bf16[32,128]{1,0:T(8,128)(2,1)S(1)}, u32[]{:S(2)}, u32[]{:S(2)}) collective-permute-start(bf16[32,128]{1,0:T(8,128)(2,1)S(1)} %get-tuple-element.33), channel_id=1, source_target_pairs={{0,24},{8,16},{16,8},{24,0},{1,25},{9,17},{17,9},{25,1},{2,26},{10... | collective-permute-start | bytes 24584 | tf_op jit(solution)/shard_map/ppermute | solution.py:20
  18.7 3.7 %collective-permute-start.8 = (bf16[32,128]{1,0:T(8,128)(2,1)S(1)}, bf16[32,128]{1,0:T(8,128)(2,1)S(1)}, u32[]{:S(2)}, u32[]{:S(2)}) collective-permute-start(bf16[32,128]{1,0:T(8,128)(2,1)S(1)} %get-tuple-element.34), channel_id=1, source_target_pairs={{0,16},{8,24},{16,0},{24,8},{1,17},{9,25},{17,1},{25,9},{2,18},{10... | collective-permute-start | bytes 24584 | tf_op jit(solution)/shard_map/ppermute | solution.py:20
  19.2 3.7 %collective-permute-start.9 = (bf16[32,128]{1,0:T(8,128)(2,1)S(1)}, bf16[32,128]{1,0:T(8,128)(2,1)S(1)}, u32[]{:S(2)}, u32[]{:S(2)}) collective-permute-start(bf16[32,128]{1,0:T(8,128)(2,1)S(1)} %get-tuple-element.35), channel_id=1, source_target_pairs={{0,8},{8,0},{16,24},{24,16},{1,9},{9,1},{17,25},{25,17},{2,10},{10... | collective-permute-start | bytes 24584 | tf_op jit(solution)/shard_map/ppermute | solution.py:20
